TPU v7x, 32 devices: a whole 2x2x4 slice. The times are simulated.
32 devices in a mesh: dp: 8 (over y, x, core), seq: 4 (over z).
Axes of the slice: x: 2, y: 2, z: 4, core: 2. Of those that a mesh axis runs over, the one named last changes fastest.
Arguments:
- tokens: bfloat16 [16, 1024, 512], P('dp', 'seq'), may hold values from -6 to 6
- memory: bfloat16 [16, 1024, 512], P('dp', 'seq'), may hold values from -6 to 6
- tgt_segments: int32 [16, 1024], P('dp'), may hold values from 0 to 2, as said below
- mem_segments: int32 [16, 1024], P('dp'), may hold values from 0 to 2, as said below
- cotangent: bfloat16 [16, 1024, 512], P('dp', 'seq'), may hold values from -6 to 6
- w_qkv: bfloat16 [512, 1536], replicated, may hold values from -0.25 to 0.25
- w_self_out: bfloat16 [512, 512], replicated, may hold values from -1.5 to 1.5
- w_cross_q: bfloat16 [512, 512], replicated, may hold values from -0.25 to 0.25
- w_cross_kv: bfloat16 [512, 1024], replicated, may hold values from -0.25 to 0.25
- w_cross_out: bfloat16 [512, 512], replicated, may hold values from -1.5 to 1.5
- w_up: bfloat16 [512, 2048], replicated, may hold values from -0.25 to 0.25
- w_down: bfloat16 [2048, 512], replicated, may hold values from -0.125 to 0.125
- ln1_gain: float32 [512], replicated, may hold values from 0.25 to 1.75
- ln1_bias: float32 [512], replicated, may hold values from -1.8 to 1.8
- ln2_gain: float32 [512], replicated, may hold values from 0.25 to 1.75
- ln2_bias: float32 [512], replicated, may hold values from -1.8 to 1.8
- ln3_gain: float32 [512], replicated, may hold values from 0.25 to 1.75
- ln3_bias: float32 [512], replicated, may hold values from -1.8 to 1.8
Outputs:
- output: bfloat16 [16, 1024, 512], P('dp', 'seq')
- grad_tokens: float32 [16, 1024, 512], P('dp', 'seq')
- grad_memory: float32 [16, 1024, 512], P('dp', 'seq')
- grad_w_qkv: float32 [512, 1536], replicated
- grad_w_self_out: float32 [512, 512], replicated
- grad_w_cross_q: float32 [512, 512], replicated
- grad_w_cross_kv: float32 [512, 1024], replicated
- grad_w_cross_out: float32 [512, 512], replicated
- grad_w_up: float32 [512, 2048], replicated
- grad_w_down: float32 [2048, 512], replicated
- grad_ln1_gain: float32 [512], replicated
- grad_ln1_bias: float32 [512], replicated
- grad_ln2_gain: float32 [512], replicated
- grad_ln2_bias: float32 [512], replicated
- grad_ln3_gain: float32 [512], replicated
- grad_ln3_bias: float32 [512], replicated
Inputs may be any that keep to these rules, and one draw needn't show every extreme that they name: `tgt_segments`: along a row the ids never fall and all three occur; document 1 begins within the row's first 256 positions and ends within its last 256. `mem_segments`: along a row the ids never fall and all three occur.
All inputs are finite; a program needn't handle non-finite values.
Results may differ from a plain program's by a relative error of at most 0.02.
Values may be sent and summed in bfloat16 or wider, within the bound.
No kernel may reach another device: no remote copies, remote signals or barrier semaphores. Data moves between devices by JAX's collectives and lax.ppermute only.
A program may use at most 128 MiB of HBM per device.

v0:
```python
import math
import jax
import jax.numpy as jnp
from jax import lax
from jax.sharding import PartitionSpec as P

HEAD_DIM = 64


def mat_dot(left, right):
    return jnp.dot(left, right, preferred_element_type=jnp.float32)


def left_dot(left, right):
    return lax.dot_general(
        left, right, (((0,), (0,)), ((), ())), preferred_element_type=jnp.float32
    )


def right_dot(left, right):
    return lax.dot_general(
        left, right, (((1,), (1,)), ((), ())), preferred_element_type=jnp.float32
    )


def layer_norm(values, gain, bias):
    centre = values - jnp.mean(values, axis=-1, keepdims=True)
    recip = lax.rsqrt(jnp.mean(centre * centre, axis=-1, keepdims=True) + 1e-05)
    normed = centre * recip
    return (normed * gain + bias, normed, recip)


def norm_back(grad_out, normed, recip, gain):
    grad_gain = jnp.sum(grad_out * normed, axis=0)
    grad_bias = jnp.sum(grad_out, axis=0)
    scaled = grad_out * gain
    grad_in = recip * (
        scaled
        - jnp.mean(scaled, axis=-1, keepdims=True)
        - normed * jnp.mean(scaled * normed, axis=-1, keepdims=True)
    )
    return (grad_in, grad_gain, grad_bias)


def causal_mask(segment_row):
    place = jnp.arange(segment_row.shape[0])
    return (place[None, :] <= place[:, None]) & (segment_row[:, None] == segment_row[None, :])


def cross_mask(tgt_row, mem_row):
    return tgt_row[:, None] == mem_row[None, :]


def masked_scores(queries, key_heads, allowed, score_scale):
    scores = (
        jnp.einsum("qhd,khd->hqk", queries, key_heads, preferred_element_type=jnp.float32)
        * score_scale
    )
    return jnp.where(allowed[None], scores, -1000000000.0)


def attend_forward(queries, key_heads, value_heads, allowed, score_scale):
    scores = masked_scores(queries, key_heads, allowed, score_scale)
    highest = jnp.max(scores, axis=-1, keepdims=True)
    expo = jnp.exp(scores - highest)
    total = jnp.sum(expo, axis=-1, keepdims=True)
    probs = (expo / total).astype(jnp.bfloat16)
    context = jnp.einsum("hqk,khd->qhd", probs, value_heads, preferred_element_type=jnp.float32)
    return (context.astype(jnp.bfloat16), highest + jnp.log(total))


def attend_backward(queries, key_heads, value_heads, log_total, d_context, allowed, score_scale):
    scores = masked_scores(queries, key_heads, allowed, score_scale)
    probs = jnp.exp(scores - log_total)
    d_values = jnp.einsum(
        "hqk,qhd->khd", probs.astype(jnp.bfloat16), d_context, preferred_element_type=jnp.float32
    ).astype(jnp.bfloat16)
    d_probs = jnp.einsum("qhd,khd->hqk", d_context, value_heads, preferred_element_type=jnp.float32)
    centre = jnp.sum(probs * d_probs, axis=-1, keepdims=True)
    d_scores = (probs * (d_probs - centre)).astype(jnp.bfloat16)
    d_queries = (
        jnp.einsum("hqk,khd->qhd", d_scores, key_heads, preferred_element_type=jnp.float32)
        * score_scale
    ).astype(jnp.bfloat16)
    d_keys = (
        jnp.einsum("hqk,qhd->khd", d_scores, queries, preferred_element_type=jnp.float32)
        * score_scale
    ).astype(jnp.bfloat16)
    return (d_queries, d_keys, d_values)


def body(
    tokens,
    memory,
    tgt_segments,
    mem_segments,
    cotangent,
    w_qkv,
    w_self_out,
    w_cross_q,
    w_cross_kv,
    w_cross_out,
    w_up,
    w_down,
    ln1_gain,
    ln1_bias,
    ln2_gain,
    ln2_bias,
    ln3_gain,
    ln3_bias,
):
    row_count, tok_local, model_width = tokens.shape
    mem_local = memory.shape[1]
    seq_parts = lax.axis_size("seq")
    head_share = model_width // seq_parts
    heads_here = head_share // HEAD_DIM
    seq_len = tgt_segments.shape[1]
    mem_len = mem_segments.shape[1]
    score_scale = 1.0 / math.sqrt(HEAD_DIM)
    token_total = row_count * tok_local
    flat_tokens = tokens.reshape(token_total, model_width)
    flat_memory = memory.reshape(row_count * mem_local, model_width)
    mixed_proj = (
        mat_dot(flat_tokens, w_qkv)
        .astype(jnp.bfloat16)
        .reshape(row_count, tok_local, 3, seq_parts, head_share)
    )
    self_heads = lax.all_to_all(mixed_proj, "seq", split_axis=3, concat_axis=1, tiled=True).reshape(
        row_count, seq_len, 3, heads_here, HEAD_DIM
    )
    memory_proj = (
        mat_dot(flat_memory, w_cross_kv)
        .astype(jnp.bfloat16)
        .reshape(row_count, mem_local, 2, seq_parts, head_share)
    )
    memory_heads = lax.all_to_all(
        memory_proj, "seq", split_axis=3, concat_axis=1, tiled=True
    ).reshape(row_count, mem_len, 2, heads_here, HEAD_DIM)
    self_q = self_heads[:, :, 0]
    self_k = self_heads[:, :, 1]
    self_v = self_heads[:, :, 2]
    memory_k = memory_heads[:, :, 0]
    memory_v = memory_heads[:, :, 1]

    def self_forward(row_item):
        queries, key_heads, value_heads, segment_row = row_item
        return attend_forward(
            queries, key_heads, value_heads, causal_mask(segment_row), score_scale
        )

    self_context, self_lse = lax.map(self_forward, (self_q, self_k, self_v, tgt_segments))
    self_back = lax.all_to_all(
        self_context.reshape(row_count, seq_len, 1, head_share),
        "seq",
        split_axis=1,
        concat_axis=2,
        tiled=True,
    )
    context_one = self_back.reshape(token_total, model_width)
    attn_one = mat_dot(context_one, w_self_out)
    norm_one, normed_one, recip_one = layer_norm(
        flat_tokens.astype(jnp.float32) + attn_one, ln1_gain, ln1_bias
    )
    norm_one_low = norm_one.astype(jnp.bfloat16)
    cross_proj = (
        mat_dot(norm_one_low, w_cross_q)
        .astype(jnp.bfloat16)
        .reshape(row_count, tok_local, 1, seq_parts, head_share)
    )
    cross_q = lax.all_to_all(cross_proj, "seq", split_axis=3, concat_axis=1, tiled=True).reshape(
        row_count, seq_len, heads_here, HEAD_DIM
    )

    def cross_forward(row_item):
        queries, key_heads, value_heads, tgt_row, mem_row = row_item
        return attend_forward(
            queries, key_heads, value_heads, cross_mask(tgt_row, mem_row), score_scale
        )

    cross_context, cross_lse = lax.map(
        cross_forward, (cross_q, memory_k, memory_v, tgt_segments, mem_segments)
    )
    cross_back = lax.all_to_all(
        cross_context.reshape(row_count, seq_len, 1, head_share),
        "seq",
        split_axis=1,
        concat_axis=2,
        tiled=True,
    )
    context_two = cross_back.reshape(token_total, model_width)
    attn_two = mat_dot(context_two, w_cross_out)
    norm_two, normed_two, recip_two = layer_norm(norm_one + attn_two, ln2_gain, ln2_bias)
    norm_two_low = norm_two.astype(jnp.bfloat16)
    pre_act = mat_dot(norm_two_low, w_up)
    sigma = jax.nn.sigmoid(pre_act)
    hidden_low = (pre_act * sigma).astype(jnp.bfloat16)
    fed = mat_dot(hidden_low, w_down)
    result, normed_three, recip_three = layer_norm(norm_two + fed, ln3_gain, ln3_bias)
    output = result.astype(jnp.bfloat16).reshape(row_count, tok_local, model_width)
    grad_out = cotangent.reshape(token_total, model_width).astype(jnp.float32)
    d_resid_three, d_gain_three, d_bias_three = norm_back(
        grad_out, normed_three, recip_three, ln3_gain
    )
    d_fed_low = d_resid_three.astype(jnp.bfloat16)
    grad_down = left_dot(hidden_low, d_fed_low)
    d_hidden = right_dot(d_fed_low, w_down)
    d_pre_low = (d_hidden * sigma * (1.0 + pre_act * (1.0 - sigma))).astype(jnp.bfloat16)
    grad_up = left_dot(norm_two_low, d_pre_low)
    d_norm_two = d_resid_three + right_dot(d_pre_low, w_up)
    d_resid_two, d_gain_two, d_bias_two = norm_back(d_norm_two, normed_two, recip_two, ln2_gain)
    d_attn_two = d_resid_two.astype(jnp.bfloat16)
    grad_cross_out = left_dot(context_two, d_attn_two)
    d_context_two = (
        right_dot(d_attn_two, w_cross_out)
        .astype(jnp.bfloat16)
        .reshape(row_count, tok_local, seq_parts, head_share)
    )
    d_cross_heads = lax.all_to_all(
        d_context_two, "seq", split_axis=2, concat_axis=1, tiled=True
    ).reshape(row_count, seq_len, heads_here, HEAD_DIM)

    def cross_backward(row_item):
        queries, key_heads, value_heads, log_total, d_context, tgt_row, mem_row = row_item
        return attend_backward(
            queries,
            key_heads,
            value_heads,
            log_total,
            d_context,
            cross_mask(tgt_row, mem_row),
            score_scale,
        )

    d_cross_q, d_mem_keys, d_mem_values = lax.map(
        cross_backward,
        (cross_q, memory_k, memory_v, cross_lse, d_cross_heads, tgt_segments, mem_segments),
    )
    d_memory_kv = jnp.stack((d_mem_keys, d_mem_values), axis=2).reshape(
        row_count, mem_len, 2, 1, head_share
    )
    back_query, back_memory = (
        lax.all_to_all(
            d_cross_q.reshape(row_count, seq_len, 1, 1, head_share),
            "seq",
            split_axis=1,
            concat_axis=3,
            tiled=True,
        ),
        lax.all_to_all(d_memory_kv, "seq", split_axis=1, concat_axis=3, tiled=True),
    )
    d_query_flat = back_query.reshape(token_total, model_width)
    d_memory_flat = back_memory.reshape(row_count * mem_local, 2 * model_width)
    grad_cross_q = left_dot(norm_one_low, d_query_flat)
    grad_cross_kv = left_dot(flat_memory, d_memory_flat)
    grad_memory = right_dot(d_memory_flat, w_cross_kv).reshape(row_count, mem_local, model_width)
    d_norm_one = d_resid_two + right_dot(d_query_flat, w_cross_q)
    d_resid_one, d_gain_one, d_bias_one = norm_back(d_norm_one, normed_one, recip_one, ln1_gain)
    d_attn_one = d_resid_one.astype(jnp.bfloat16)
    grad_self_out = left_dot(context_one, d_attn_one)
    d_context_one = (
        right_dot(d_attn_one, w_self_out)
        .astype(jnp.bfloat16)
        .reshape(row_count, tok_local, seq_parts, head_share)
    )
    d_self_heads = lax.all_to_all(
        d_context_one, "seq", split_axis=2, concat_axis=1, tiled=True
    ).reshape(row_count, seq_len, heads_here, HEAD_DIM)

    def self_backward(row_item):
        queries, key_heads, value_heads, log_total, d_context, segment_row = row_item
        return attend_backward(
            queries,
            key_heads,
            value_heads,
            log_total,
            d_context,
            causal_mask(segment_row),
            score_scale,
        )

    d_self_q, d_self_k, d_self_v = lax.map(
        self_backward, (self_q, self_k, self_v, self_lse, d_self_heads, tgt_segments)
    )
    d_mixed = jnp.stack((d_self_q, d_self_k, d_self_v), axis=2).reshape(
        row_count, seq_len, 3, 1, head_share
    )
    back_mixed = lax.all_to_all(d_mixed, "seq", split_axis=1, concat_axis=3, tiled=True).reshape(
        token_total, 3 * model_width
    )
    grad_qkv = left_dot(flat_tokens, back_mixed)
    grad_tokens = (d_resid_one + right_dot(back_mixed, w_qkv)).reshape(
        row_count, tok_local, model_width
    )
    summed = lax.psum(
        (
            grad_qkv,
            grad_self_out,
            grad_cross_q,
            grad_cross_kv,
            grad_cross_out,
            grad_up,
            grad_down,
            d_gain_one,
            d_bias_one,
            d_gain_two,
            d_bias_two,
            d_gain_three,
            d_bias_three,
        ),
        ("dp", "seq"),
    )
    return (
        output,
        grad_tokens,
        grad_memory,
        summed[0],
        summed[1],
        summed[2],
        summed[3],
        summed[4],
        summed[5],
        summed[6],
        summed[7],
        summed[8],
        summed[9],
        summed[10],
        summed[11],
        summed[12],
    )


def solution(mesh):
    return jax.shard_map(
        body,
        mesh=mesh,
        in_specs=(
            P("dp", "seq", None),
            P("dp", "seq", None),
            P("dp", None),
            P("dp", None),
            P("dp", "seq", None),
            P(),
            P(),
            P(),
            P(),
            P(),
            P(),
            P(),
            P(),
            P(),
            P(),
            P(),
            P(),
            P(),
        ),
        out_specs=(
            P("dp", "seq", None),
            P("dp", "seq", None),
            P("dp", "seq", None),
            P(),
            P(),
            P(),
            P(),
            P(),
            P(),
            P(),
            P(),
            P(),
            P(),
            P(),
            P(),
            P(),
        ),
        check_vma=False,
    )
```

profile of v0, /device:TPU:0, one launch (start us, length us, event | category | flops | bytes accessed | tf_op | source)
XLA Modules:
  0.0 717.0 jit_solution(7663693203559814328)
XLA Ops:
  7.2 3.8 convolution_convert_fusion
  11.0 3.9 reshape.401
  15.0 2.9 copy.196
  17.9 6.3 all-to-all-start
  24.2 37.1 %all-to-all-done = bf16[2,256,3,4,128]{4,1,2,0,3:T(8,128)(2,1)} async-done(((bf16[2,256,3,4,128]{4,1,2,0,3:T(8,128)(2,1)}), bf16[2,256,3,4,128]{4,1,2,0,3:T(8,128)(2,1)}, u32[]{:S(2)}, u32[]{:S(2)}) %all-to-all-start) | async-done | bytes 1572896 | tf_op jit(solution)/shard_map/all_to_all | solution.py:128
  61.3 3.8 copy.197
  65.0 3.8 reshape.402
  72.0 16.4 %while.52 = (s32[]{:T(128)}, bf16[2,1024,2,64]{1,3,2,0:T(8,128)(2,1)}, f32[2,2,1024,1]{2,1,3,0:T(2,128)S(1)}, bf16[2,1024,2,64]{1,3,2,0:T(8,128)(2,1)}, s32[2,10...) while((s32[]{:T(128)}, ...), condition=%wide.region_3.4_spmd, body=%wide.region_0.3_spmd.sunk | while | flops 565311488 | bytes 36780216 | solution.py:151
  76.6 2.8 fusion.227
  84.8 2.8 fusion.227
  90.7 4.1 all-to-all-start.1
  94.8 3.1 convolution_convert_fusion.1
  100.5 3.0 copy.201
  103.5 5.4 all-to-all-done.1
  108.9 4.3 all-to-all-start.2
  122.7 15.7 %all-to-all-done.2 = bf16[2,256,2,4,128]{4,2,1,0,3:T(2,128)(2,1)} async-done(((bf16[2,256,2,4,128]{4,2,1,0,3:T(2,128)(2,1)}), bf16[2,256,2,4,128]{4,2,1,0,3:T(2,128)(2,1)}, u32[]{:S(2)}, u32[]{:S(2)}) %all-to-all-start.2) | async-done | bytes 1048608 | tf_op jit(solution)/shard_map/all_to_all | solution.py:136
  138.4 4.4 all-to-all-start.3
  142.9 3.8 copy.202
  151.5 5.4 all-to-all-done.3
  162.1 18.5 %while.53 = (s32[]{:T(128)}, bf16[2,1024,2,64]{1,3,2,0:T(8,128)(2,1)}, f32[2,2,1024,1]{2,1,3,0:T(2,128)S(1)}, bf16[2,1024,2,64]{1,3,2,0:T(8,128)(2,1)}, s32[2,10...) while((s32[]{:T(128)}, ...), condition=%wide.region_9.10_spmd, body=%wide.region_6.9_spmd.sunk | while | flops 563214336 | bytes 36792512 | solution.py:180
  162.8 2.9 fusion.229
  172.0 2.9 fusion.229
  177.0 2.8 fusion.231
  182.6 4.8 all-to-all-start.4
  189.4 12.1 %all-to-all-done.4 = bf16[2,1024,1,128]{3,0,2,1:T(2,128)(2,1)} async-done(((bf16[2,1024,1,128]{3,0,2,1:T(2,128)(2,1)}), bf16[2,1024,1,128]{3,0,2,1:T(2,128)(2,1)}, u32[]{:S(2)}, u32[]{:S(2)}) %all-to-all-start.4) | async-done | bytes 524320 | tf_op jit(solution)/shard_map/all_to_all | solution.py:183
  221.2 4.3 all-to-all-start.5
  225.5 14.1 %all-to-all-done.5 = bf16[2,256,4,128]{3,1,0,2:T(8,128)(2,1)} async-done(((bf16[2,256,4,128]{3,1,0,2:T(8,128)(2,1)}), bf16[2,256,4,128]{3,1,0,2:T(8,128)(2,1)}, u32[]{:S(2)}, u32[]{:S(2)}) %all-to-all-start.5) | async-done | bytes 524320 | tf_op jit(solution)/shard_map/all_to_all | solution.py:218
  246.6 27.1 %while.54 = (s32[]{:T(128)}, bf16[2,1024,2,64]{1,3,2,0:T(8,128)(2,1)}, bf16[2,1024,2,64]{1,3,2,0:T(8,128)(2,1)}, bf16[2,1024,2,64]{1,3,2,0:T(8,128)(2,1)}, bf16[...) while((s32[]{:T(128)}, ...), condition=%wide.region_20.21_spmd, body=%wide.region_18.20_spmd.sunk | while | flops 1375336448 | bytes 86594928 | solution.py:234
  248.6 3.0 multiply_reduce_fusion.13
  262.2 3.0 multiply_reduce_fusion.13
  275.1 16.4 %all_to_all.150 = bf16[2,1024,1,1,128]{4,0,3,2,1:T(2,128)(2,1)S(1)} all-to-all(bf16[2,1024,1,1,128]{4,0,3,2,1:T(2,128)(2,1)S(1)} %copy.210), channel_id=1, replica_groups=mesh['dp'=8,'seq'=4] {'seq'}, dimensions={1} | all-to-all | bytes 1048576 | tf_op jit(solution)/shard_map/all_to_all | solution.py:242
  296.0 4.1 all-to-all-start.7
  303.5 10.2 %all-to-all-done.7 = bf16[2,256,4,128]{3,1,0,2:T(8,128)(2,1)} async-done(((bf16[2,256,4,128]{3,1,0,2:T(8,128)(2,1)}), bf16[2,256,4,128]{3,1,0,2:T(8,128)(2,1)}, u32[]{:S(2)}, u32[]{:S(2)}) %all-to-all-start.7) | async-done | bytes 524320 | tf_op jit(solution)/shard_map/all_to_all | solution.py:265
  313.7 4.5 all-to-all-start.9
  323.4 27.0 %while.55 = (s32[]{:T(128)}, bf16[2,1024,2,64]{1,3,2,0:T(8,128)(2,1)}, bf16[2,1024,2,64]{1,3,2,0:T(8,128)(2,1)}, bf16[2,1024,2,64]{1,3,2,0:T(8,128)(2,1)}, bf16[...) while((s32[]{:T(128)}, ...), condition=%wide.region_25.26_spmd, body=%wide.region_23.25_spmd.sunk | while | flops 1377433600 | bytes 86582632 | solution.py:281
  325.4 3.0 multiply_reduce_fusion.14
  338.9 3.0 multiply_reduce_fusion.14
  353.2 5.0 copy.215
  358.2 5.1 all-to-all-start.8
  366.2 5.2 fusion.153
  371.4 3.5 fusion.150
  383.1 16.2 %all-to-all-done.8 = bf16[2,1024,3,1,128]{4,0,3,2,1:T(2,128)(2,1)} async-done(((bf16[2,1024,3,1,128]{4,0,3,2,1:T(2,128)(2,1)}), bf16[2,1024,3,1,128]{4,0,3,2,1:T(2,128)(2,1)}, u32[]{:S(2)}, u32[]{:S(2)}) %all-to-all-start.8) | async-done | bytes 1572896 | tf_op jit(solution)/shard_map/all_to_all | solution.py:287
  403.3 2.8 reshape.419
  409.5 40.1 %all-reduce = (f32[512]{0:T(512)}, f32[512]{0:T(512)}, f32[512]{0:T(512)}, f32[512]{0:T(512)}, f32[512]{0:T(512)}, /*index=5*/f32[512]{0:T(512)}) all-reduce(f32[512]{0:T(512)S(1)} %get-tuple-element.334, f32[512]{0:T(512)S(1)} %get-tuple-element.341, f32[512]{0:T(512)S(1)} %copy-done.74, ...), channel_id=1, replica_groups=mesh['dp'=8,'seq'=4] {'dp','seq'}, use_global_device_ids=true, to_apply=%region_34.35 | all-reduce | flops 3072 | bytes 24576 | tf_op jit(solution)/shard_map/psum | solution.py:294
  451.2 3.3 fusion.120
  454.5 3.8 convolution_add_fusion.3
  458.3 234.8 %all-reduce.4.cloned.1.call-done = (f32[512,1536]{0,1:T(8,128)}, f32[512,512]{1,0:T(8,128)}, f32[512,512]{1,0:T(8,128)}, f32[512,1024]{0,1:T(8,128)}, f32[512,51...) async-done(((f32[512,1536]{0,1:T(8,128)}, f32[512,512]{1,0:T(8,128)}, f32[512,512]{1,0:T(8,128)}, f32[512,1024]{0,1:T(8,128)}, f32[512,512]{1,0:T(8,128)}, ...) | async-done | bytes 16777232 | tf_op jit(solution)/shard_map/psum | solution.py:294
  693.1 3.7 copy.222
  (341 shorter events, 170.1 us)
Async XLA Ops:
  7.2 198.6 %copy-start = (bf16[512,2048]{1,0:T(8,128)(2,1)S(1)}, bf16[512,2048]{1,0:T(8,128)(2,1)}, u32[]{:S(2)}) copy-start(bf16[512,2048]{1,0:T(8,128)(2,1)} %param.36) | copy-start | bytes 6291460
  17.9 43.4 %all-to-all-start = ((bf16[2,256,3,4,128]{4,1,2,0,3:T(8,128)(2,1)}), bf16[2,256,3,4,128]{4,1,2,0,3:T(8,128)(2,1)}, u32[]{:S(2)}, u32[]{:S(2)}) async-start(bf16[2,256,3,4,128]{4,1,2,0,3:T(8,128)(2,1)} %copy.196), calls=%async_computation | async-start | bytes 3145728 | tf_op jit(solution)/shard_map/all_to_all | solution.py:128
  65.0 7.0 copy-start.55
  88.4 15.1 %copy-start.5 = (bf16[2,1024,2,64]{1,3,2,0:T(8,128)(2,1)}, bf16[2,1024,2,64]{1,3,2,0:T(8,128)(2,1)S(1)}, u32[]{:S(2)}) copy-start(bf16[2,1024,2,64]{1,3,2,0:T(8,128)(2,1)S(1)} %get-tuple-element.855) | copy-start | bytes 1572868
  88.4 15.1 %copy-start.7 = (bf16[2,1024,2,64]{1,3,2,0:T(8,128)(2,1)}, bf16[2,1024,2,64]{1,3,2,0:T(8,128)(2,1)S(1)}, u32[]{:S(2)}) copy-start(bf16[2,1024,2,64]{1,3,2,0:T(8,128)(2,1)S(1)} %get-tuple-element.856) | copy-start | bytes 1572868
  88.4 15.1 %copy-start.59 = (f32[2,2,1024,1]{2,1,3,0:T(2,128)}, f32[2,2,1024,1]{2,1,3,0:T(2,128)S(1)}, u32[]{:S(2)}) copy-start(f32[2,2,1024,1]{2,1,3,0:T(2,128)S(1)} %get-tuple-element.796) | copy-start | bytes 49156
  90.7 18.2 %all-to-all-start.1 = ((bf16[2,1024,1,128]{3,0,2,1:T(2,128)(2,1)}), bf16[2,1024,1,128]{3,0,2,1:T(2,128)(2,1)}, u32[]{:S(2)}, u32[]{:S(2)}) async-start(bf16[2,1024,1,128]{3,0,2,1:T(2,128)(2,1)} %copy.198), calls=%async_computation.1 | async-start | bytes 1048576 | tf_op jit(solution)/shard_map/all_to_all | solution.py:152
  103.5 14.1 %copy-start.70 = (f32[512]{0:T(512)S(1)}, f32[512]{0:T(512)}, u32[]{:S(2)}) copy-start(f32[512]{0:T(512)} %param.38) | copy-start | bytes 6148
  103.5 14.1 %copy-start.76 = (f32[512]{0:T(512)S(1)}, f32[512]{0:T(512)}, u32[]{:S(2)}) copy-start(f32[512]{0:T(512)} %param.39) | copy-start | bytes 6148
  108.9 29.5 %all-to-all-start.2 = ((bf16[2,256,2,4,128]{4,2,1,0,3:T(2,128)(2,1)}), bf16[2,256,2,4,128]{4,2,1,0,3:T(2,128)(2,1)}, u32[]{:S(2)}, u32[]{:S(2)}) async-start(bf16[2,256,2,4,128]{4,2,1,0,3:T(2,128)(2,1)} %copy.201), calls=%async_computation.2 | async-start | bytes 2097152 | tf_op jit(solution)/shard_map/all_to_all | solution.py:136
  113.2 4.4 copy-start.56
  138.4 18.5 %all-to-all-start.3 = ((bf16[2,256,1,4,128]{4,1,0,2,3:T(8,128)(2,1)}), bf16[2,256,1,4,128]{4,1,0,2,3:T(8,128)(2,1)}, u32[]{:S(2)}, u32[]{:S(2)}) async-start(bf16[2,256,1,4,128]{4,1,0,2,3:T(8,128)(2,1)} %copy.203), calls=%async_computation.3 | async-start | bytes 1048576 | tf_op jit(solution)/shard_map/all_to_all | solution.py:170
  142.9 19.2 %copy-start.58 = (s32[2,1024]{1,0:T(2,128)S(1)}, s32[2,1024]{1,0:T(2,128)}, u32[]{:S(2)}) copy-start(s32[2,1024]{1,0:T(2,128)} %param.29) | copy-start | bytes 24580
  162.1 25.4 %copy-start.69 = (f32[512]{0:T(512)S(1)}, f32[512]{0:T(512)}, u32[]{:S(2)}) copy-start(f32[512]{0:T(512)} %param.42) | copy-start | bytes 6148
  182.6 23.2 %copy-start.65 = (f32[512]{0:T(512)S(1)}, f32[512]{0:T(512)}, u32[]{:S(2)}) copy-start(f32[512]{0:T(512)} %param.40) | copy-start | bytes 6148
  182.6 23.2 %copy-start.67 = (f32[512]{0:T(512)S(1)}, f32[512]{0:T(512)}, u32[]{:S(2)}) copy-start(f32[512]{0:T(512)} %param.41) | copy-start | bytes 6148
  182.6 18.9 %all-to-all-start.4 = ((bf16[2,1024,1,128]{3,0,2,1:T(2,128)(2,1)}), bf16[2,1024,1,128]{3,0,2,1:T(2,128)(2,1)}, u32[]{:S(2)}, u32[]{:S(2)}) async-start(bf16[2,1024,1,128]{3,0,2,1:T(2,128)(2,1)} %copy.205), calls=%async_computation.4 | async-start | bytes 1048576 | tf_op jit(solution)/shard_map/all_to_all | solution.py:183
  205.5 10.1 %copy-start.2 = (f32[512,512]{1,0:T(8,128)}, f32[512,512]{1,0:T(8,128)S(1)}, u32[]{:S(2)}) copy-start(f32[512,512]{1,0:T(8,128)S(1)} %get-tuple-element.451) | copy-start | bytes 3145732
  205.5 10.1 %copy-start.61 = (f32[512]{0:T(512)}, f32[512]{0:T(512)S(1)}, u32[]{:S(2)}) copy-start(f32[512]{0:T(512)S(1)} %broadcast_multiply_fusion.6) | copy-start | bytes 6148
  205.8 9.8 %copy-start.63 = (f32[512]{0:T(512)}, f32[512]{0:T(512)S(1)}, u32[]{:S(2)}) copy-start(f32[512]{0:T(512)S(1)} %add_rsqrt_fusion.1) | copy-start | bytes 6148
  216.0 29.8 %copy-start.10 = (f32[512,512]{1,0:T(8,128)}, f32[512,512]{1,0:T(8,128)S(1)}, u32[]{:S(2)}) copy-start(f32[512,512]{1,0:T(8,128)S(1)} %subtract_multiply_fusion.1) | copy-start | bytes 3145732
  216.0 30.6 %copy-start.4 = (bf16[2,1024,2,64]{1,3,2,0:T(8,128)(2,1)S(1)}, bf16[2,1024,2,64]{1,3,2,0:T(8,128)(2,1)}, u32[]{:S(2)}) copy-start(bf16[2,1024,2,64]{1,3,2,0:T(8,128)(2,1)} %get-tuple-element.854) | copy-start | bytes 1572868
  216.0 30.6 %copy-start.9 = (bf16[2,1024,2,64]{1,3,2,0:T(8,128)(2,1)S(1)}, bf16[2,1024,2,64]{1,3,2,0:T(8,128)(2,1)}, u32[]{:S(2)}) copy-start(bf16[2,1024,2,64]{1,3,2,0:T(8,128)(2,1)} %get-tuple-element.857) | copy-start | bytes 1572868
  221.2 18.4 %all-to-all-start.5 = ((bf16[2,256,4,128]{3,1,0,2:T(8,128)(2,1)}), bf16[2,256,4,128]{3,1,0,2:T(8,128)(2,1)}, u32[]{:S(2)}, u32[]{:S(2)}) async-start(bf16[2,256,4,128]{3,1,0,2:T(8,128)(2,1)} %copy.208), calls=%async_computation.5 | async-start | bytes 1048576 | tf_op jit(solution)/shard_map/all_to_all | solution.py:218
  273.7 18.3 %copy-start.11 = (f32[512,512]{1,0:T(8,128)S(1)}, f32[512,512]{1,0:T(8,128)}, u32[]{:S(2)}) copy-start(f32[512,512]{1,0:T(8,128)} %copy-done.10) | copy-start | bytes 3145732
  294.5 5.7 copy-start.13
  296.0 17.8 %all-to-all-start.7 = ((bf16[2,256,4,128]{3,1,0,2:T(8,128)(2,1)}), bf16[2,256,4,128]{3,1,0,2:T(8,128)(2,1)}, u32[]{:S(2)}, u32[]{:S(2)}) async-start(bf16[2,256,4,128]{3,1,0,2:T(8,128)(2,1)} %copy.213), calls=%async_computation.7 | async-start | bytes 1048576 | tf_op jit(solution)/shard_map/all_to_all | solution.py:265
  301.4 21.9 %copy-start.6 = (bf16[2,1024,2,64]{1,3,2,0:T(8,128)(2,1)S(1)}, bf16[2,1024,2,64]{1,3,2,0:T(8,128)(2,1)}, u32[]{:S(2)}) copy-start(bf16[2,1024,2,64]{1,3,2,0:T(8,128)(2,1)} %copy-done.5) | copy-start | bytes 1572868
  301.4 21.9 %copy-start.8 = (bf16[2,1024,2,64]{1,3,2,0:T(8,128)(2,1)S(1)}, bf16[2,1024,2,64]{1,3,2,0:T(8,128)(2,1)}, u32[]{:S(2)}) copy-start(bf16[2,1024,2,64]{1,3,2,0:T(8,128)(2,1)} %copy-done.7) | copy-start | bytes 1572868
  301.5 21.9 %copy-start.60 = (f32[2,2,1024,1]{2,1,3,0:T(2,128)S(1)}, f32[2,2,1024,1]{2,1,3,0:T(2,128)}, u32[]{:S(2)}) copy-start(f32[2,2,1024,1]{2,1,3,0:T(2,128)} %copy-done.59) | copy-start | bytes 49156
  313.7 44.5 %all-to-all-start.9 = ((bf16[2,1024,2,1,128]{4,0,3,2,1:T(2,128)(2,1)}), bf16[2,1024,2,1,128]{4,0,3,2,1:T(2,128)(2,1)}, u32[]{:S(2)}, u32[]{:S(2)}) async-start(bf16[2,1024,2,1,128]{4,0,3,2,1:T(2,128)(2,1)} %copy.218), calls=%async_computation.9 | async-start | bytes 2097152 | tf_op jit(solution)/shard_map/all_to_all | solution.py:249
  350.4 13.3 %copy-start.12 = (f32[512,512]{1,0:T(8,128)S(1)}, f32[512,512]{1,0:T(8,128)}, u32[]{:S(2)}) copy-start(f32[512,512]{1,0:T(8,128)} %copy-done.10) | copy-start | bytes 3145732
  353.2 13.0 %copy-start.3 = (f32[512,512]{1,0:T(8,128)S(1)}, f32[512,512]{1,0:T(8,128)}, u32[]{:S(2)}) copy-start(f32[512,512]{1,0:T(8,128)} %copy-done.2) | copy-start | bytes 3145732
  353.2 13.0 %copy-start.62 = (f32[512]{0:T(512)S(1)}, f32[512]{0:T(512)}, u32[]{:S(2)}) copy-start(f32[512]{0:T(512)} %copy-done.61) | copy-start | bytes 6148
  353.2 13.0 %copy-start.64 = (f32[512]{0:T(512)S(1)}, f32[512]{0:T(512)}, u32[]{:S(2)}) copy-start(f32[512]{0:T(512)} %copy-done.63) | copy-start | bytes 6148
  353.2 13.0 %copy-start.66 = (f32[512]{0:T(512)S(1)}, f32[512]{0:T(512)}, u32[]{:S(2)}) copy-start(f32[512]{0:T(512)} %param.40) | copy-start | bytes 6148
  353.2 13.0 %copy-start.68 = (f32[512]{0:T(512)S(1)}, f32[512]{0:T(512)}, u32[]{:S(2)}) copy-start(f32[512]{0:T(512)} %param.41) | copy-start | bytes 6148
  358.2 41.1 %all-to-all-start.8 = ((bf16[2,1024,3,1,128]{4,0,3,2,1:T(2,128)(2,1)}), bf16[2,1024,3,1,128]{4,0,3,2,1:T(2,128)(2,1)}, u32[]{:S(2)}, u32[]{:S(2)}) async-start(bf16[2,1024,3,1,128]{4,0,3,2,1:T(2,128)(2,1)} %copy.215), calls=%async_computation.8 | async-start | bytes 3145728 | tf_op jit(solution)/shard_map/all_to_all | solution.py:287
  363.3 329.8 %all-reduce.4.cloned.1.call-start = ((), (), s32[]{:S(2)}) async-start(), calls=%async_computation.10 | async-start | bytes 33554432 | tf_op jit(solution)/shard_map/psum | solution.py:294
  366.2 5.2 copy-start.26
  366.2 5.2 copy-start.53
  371.4 4.9 copy-start.30
  371.4 4.9 copy-start.77
  376.3 4.6 copy-start.57
  383.1 23.1 %copy-start.51 = (bf16[2,256,512]{2,1,0:T(8,128)(2,1)S(1)}, bf16[2,256,512]{2,1,0:T(8,128)(2,1)}, u32[]{:S(2)}) copy-start(bf16[2,256,512]{2,1,0:T(8,128)(2,1)} %param.26) | copy-start | bytes 1572868
  696.7 6.5 copy-start.54
  698.6 5.7 copy-start.28
  704.2 5.7 copy-start.1
  (63 other events, 131.1 us)
Sparse Core Ops, SparseCore 0:
  409.0 284.0 all-reduce.3
where the time goes:
time: 728 us; the launch traced here: 717 us
  waiting for transfers between devices  351 us (48%)
  local copies, waits for them, and re-layouts  112 us (15%)
  matrix products  105 us (14%)
  blocking collectives  56.5 us (8%)
  starting transfers between devices  42.4 us (6%)
  other arithmetic  33.6 us (5%)
  between operations  14.9 us (2%)
    psum x1, waiting for transfers between devices, body(): lax.psum((grad_qkv, grad_self_out, grad_cross_q, grad_cross_kv, grad_cros...  235 us
    psum x1, blocking collectives, body(): lax.psum((grad_qkv, grad_self_out, grad_cross_q, grad_cross_kv, grad_cros...  40.1 us
    all_to_all x1, waiting for transfers between devices, body(): lax.all_to_all(mixed_proj, 'seq', split_axis=3, concat_axis=1, tiled=True)  37.1 us
    unnamed x122, local copies, waits for them, and re-layouts  19.7 us
    dot_general x7, matrix products, left_dot(): lax.dot_general(left, right, (((0,), (0,)), ((), ())), preferred_element_...  19 us
    all_to_all x1, blocking collectives, body(): lax.all_to_all(d_cross_q.reshape(row_count, seq_len, 1, 1, head_share), '...  16.4 us
    all_to_all x1, waiting for transfers between devices, body(): lax.all_to_all(d_mixed, 'seq', split_axis=1, concat_axis=3, tiled=True)  16.2 us
    all_to_all x1, waiting for transfers between devices, body(): lax.all_to_all(memory_proj, 'seq', split_axis=3, concat_axis=1, tiled=True)  15.7 us
  transfers between devices with their start and end apart: 10, of which 9 were waited for; matrix products, arithmetic and copies ran while one was open for 14% of the time, Pallas kernels for 0%

commit v1 on v0

--- a/solution.py
+++ b/solution.py
@@ -5,6 +5,29 @@
 from jax.sharding import PartitionSpec as P
 
 HEAD_DIM = 64
+
+
+def split_up(value, dim, size):
+    dims = value.shape
+    blocks = value.reshape(*dims[:dim], size, dims[dim] // size, *dims[dim + 1 :])
+    return jnp.moveaxis(blocks, dim, 0)
+
+
+def in_order(tiles, dim):
+    lengths = list(tiles.shape[1:])
+    lengths[dim] *= tiles.shape[0]
+    return jnp.moveaxis(tiles, 0, dim).reshape(lengths)
+
+
+def exchange_directly(x, axis, split_dim, concat_dim):
+    devices, index = (lax.axis_size(axis), lax.axis_index(axis))
+    parts = split_up(x, split_dim, devices)
+    done = [parts[index]]
+    for step in range(1, devices):
+        sent = parts[(index + step) % devices]
+        done.append(lax.ppermute(sent, axis, [(i, (i + step) % devices) for i in range(devices)]))
+    parts = jnp.stack(done)[(index - jnp.arange(devices)) % devices]
+    return in_order(parts, concat_dim)
 
 
 def mat_dot(left, right):
@@ -125,7 +148,7 @@
         .astype(jnp.bfloat16)
         .reshape(row_count, tok_local, 3, seq_parts, head_share)
     )
-    self_heads = lax.all_to_all(mixed_proj, "seq", split_axis=3, concat_axis=1, tiled=True).reshape(
+    self_heads = exchange_directly(mixed_proj, "seq", 3, 1).reshape(
         row_count, seq_len, 3, heads_here, HEAD_DIM
     )
     memory_proj = (

time: 728 us -> 737 us (1.012)
    all_to_all x1 -> x0, waiting for transfers between devices: 37.1 us -> none  [body(): lax.all_to_all(mixed_proj, 'seq', split_axis=3, concat_axis=1, tiled=True)]
    ppermute x0 -> x3, waiting for transfers between devices: none -> 31.1 us  [exchange_directly(): lax.ppermute(sent, axis, [(i, (i + step) % devices) for i in range(device...]
    another operation x10 -> x13, local copies, waits for them, and re-layouts: 6.96 us -> 21.2 us
    reshape x3 -> x0, local copies, waits for them, and re-layouts: 10.6 us -> none  [the longest x2 6.83 us: body(): mixed_proj = mat_dot(flat_tokens, w_qkv).astype(jnp.bfloat16).reshape(row...]
    unnamed x122 -> x120, local copies, waits for them, and re-layouts: 19.7 us -> 22.2 us
  transfers between devices with their start and end apart: 10 -> 12, of which waited for: 9 -> 10; matrix products, arithmetic and copies ran while one was open for 14% -> 13% of each run, Pallas kernels for 0% -> 0%
where the time goes in v1:
time: 737 us; the launch traced here: 727 us
  waiting for transfers between devices  348 us (47%)
  local copies, waits for them, and re-layouts  119 us (16%)
  matrix products  109 us (15%)
  blocking collectives  56.5 us (8%)
  starting transfers between devices  42.7 us (6%)
  other arithmetic  36.1 us (5%)
  between operations  15 us (2%)
    psum x1, waiting for transfers between devices, body(): lax.psum((grad_qkv, grad_self_out, grad_cross_q, grad_cross_kv, grad_cros...  235 us
    psum x1, blocking collectives, body(): lax.psum((grad_qkv, grad_self_out, grad_cross_q, grad_cross_kv, grad_cros...  40.1 us
    ppermute x3, waiting for transfers between devices, exchange_directly(): lax.ppermute(sent, axis, [(i, (i + step) % devices) for i in range(device...  31.1 us
    unnamed x120, local copies, waits for them, and re-layouts  22.2 us
    dot_general x7, matrix products, left_dot(): lax.dot_general(left, right, (((0,), (0,)), ((), ())), preferred_element_...  19 us
    dot_general x8, matrix products, masked_scores(): jnp.einsum('qhd,khd->hqk', queries, key_heads, preferred_element_type=jnp...  16.9 us
    all_to_all x1, blocking collectives, body(): lax.all_to_all(d_cross_q.reshape(row_count, seq_len, 1, 1, head_share), '...  16.4 us
    all_to_all x1, waiting for transfers between devices, body(): lax.all_to_all(d_mixed, 'seq', split_axis=1, concat_axis=3, tiled=True)  16.2 us
  transfers between devices with their start and end apart: 12, of which 10 were waited for; matrix products, arithmetic and copies ran while one was open for 13% of the time, Pallas kernels for 0%

profile of v1, /device:TPU:0, one launch (start us, length us, event | category | flops | bytes accessed | tf_op | source)
XLA Modules:
  0.0 727.0 jit_solution(14503125099861639045)
XLA Ops:
  7.2 3.8 convolution_convert_fusion
  11.1 3.9 reshape_reshape.6
  15.0 6.5 constant_dynamic-slice_fusion.9
  22.3 5.0 collective-permute-start.2
  30.1 7.2 collective-permute-done.2
  37.3 23.9 %collective-permute-done.1 = bf16[2,256,3,1,128]{4,1,2,0,3:T(8,128)(2,1)} collective-permute-done((bf16[2,256,3,1,128]{4,1,2,0,3:T(8,128)(2,1)}, bf16[2,256,3,1,128]{4,1,2,0,3:T(8,128)(2,1)}, u32[]{:S(2)}, u32[]{:S(2)}) %collective-permute-start.1) | collective-permute-done | bytes 393248 | tf_op jit(solution)/shard_map/ppermute | solution.py:28
  63.7 3.3 gather_fusion
  67.0 3.8 copy.198
  70.7 3.8 reshape_reshape.7
  77.9 18.4 %while.52 = (s32[]{:T(128)}, bf16[2,1024,2,64]{1,3,2,0:T(8,128)(2,1)}, f32[2,2,1024,1]{2,1,3,0:T(2,128)S(1)}, bf16[2,1024,2,64]{1,3,2,0:T(8,128)(2,1)}, s32[2,10...) while((s32[]{:T(128)}, ...), condition=%wide.region_3.4_spmd, body=%wide.region_0.3_spmd.sunk | while | flops 565311488 | bytes 36780216 | solution.py:174
  78.6 2.9 fusion.227
  87.7 2.9 fusion.227
  98.3 5.1 all-to-all-start
  103.4 3.1 convolution_convert_fusion.1
  110.1 8.6 %all-to-all-done = bf16[2,1024,1,128]{3,0,2,1:T(2,128)(2,1)} async-done(((bf16[2,1024,1,128]{3,0,2,1:T(2,128)(2,1)}), bf16[2,1024,1,128]{3,0,2,1:T(2,128)(2,1)}, u32[]{:S(2)}, u32[]{:S(2)}) %all-to-all-start) | async-done | bytes 524320 | tf_op jit(solution)/shard_map/all_to_all | solution.py:175
  118.7 4.2 all-to-all-start.1
  133.5 15.3 %all-to-all-done.1 = bf16[2,256,2,4,128]{4,2,1,0,3:T(2,128)(2,1)} async-done(((bf16[2,256,2,4,128]{4,2,1,0,3:T(2,128)(2,1)}), bf16[2,256,2,4,128]{4,2,1,0,3:T(2,128)(2,1)}, u32[]{:S(2)}, u32[]{:S(2)}) %all-to-all-start.1) | async-done | bytes 1048608 | tf_op jit(solution)/shard_map/all_to_all | solution.py:159
  148.8 4.1 all-to-all-start.2
  153.0 3.8 copy.203
  161.6 5.4 all-to-all-done.2
  172.2 18.5 %while.53 = (s32[]{:T(128)}, bf16[2,1024,2,64]{1,3,2,0:T(8,128)(2,1)}, f32[2,2,1024,1]{2,1,3,0:T(2,128)S(1)}, bf16[2,1024,2,64]{1,3,2,0:T(8,128)(2,1)}, s32[2,10...) while((s32[]{:T(128)}, ...), condition=%wide.region_9.10_spmd, body=%wide.region_6.9_spmd.sunk | while | flops 563214336 | bytes 36792512 | solution.py:203
  172.9 2.9 fusion.231
  182.1 2.9 fusion.231
  192.7 4.8 all-to-all-start.3
  199.4 12.1 %all-to-all-done.3 = bf16[2,1024,1,128]{3,0,2,1:T(2,128)(2,1)} async-done(((bf16[2,1024,1,128]{3,0,2,1:T(2,128)(2,1)}), bf16[2,1024,1,128]{3,0,2,1:T(2,128)(2,1)}, u32[]{:S(2)}, u32[]{:S(2)}) %all-to-all-start.3) | async-done | bytes 524320 | tf_op jit(solution)/shard_map/all_to_all | solution.py:206
  231.3 4.3 all-to-all-start.4
  235.6 14.1 %all-to-all-done.4 = bf16[2,256,4,128]{3,1,0,2:T(8,128)(2,1)} async-done(((bf16[2,256,4,128]{3,1,0,2:T(8,128)(2,1)}), bf16[2,256,4,128]{3,1,0,2:T(8,128)(2,1)}, u32[]{:S(2)}, u32[]{:S(2)}) %all-to-all-start.4) | async-done | bytes 524320 | tf_op jit(solution)/shard_map/all_to_all | solution.py:241
  256.6 27.1 %while.54 = (s32[]{:T(128)}, bf16[2,1024,2,64]{1,3,2,0:T(8,128)(2,1)}, bf16[2,1024,2,64]{1,3,2,0:T(8,128)(2,1)}, bf16[2,1024,2,64]{1,3,2,0:T(8,128)(2,1)}, bf16[...) while((s32[]{:T(128)}, ...), condition=%wide.region_20.21_spmd, body=%wide.region_18.20_spmd.sunk | while | flops 1375336448 | bytes 86594928 | solution.py:257
  258.7 3.0 multiply_reduce_fusion.13
  272.2 3.0 multiply_reduce_fusion.13
  285.2 16.4 %all_to_all.135 = bf16[2,1024,1,1,128]{4,0,3,2,1:T(2,128)(2,1)S(1)} all-to-all(bf16[2,1024,1,1,128]{4,0,3,2,1:T(2,128)(2,1)S(1)} %copy.211), channel_id=1, replica_groups=mesh['dp'=8,'seq'=4] {'seq'}, dimensions={1} | all-to-all | bytes 1048576 | tf_op jit(solution)/shard_map/all_to_all | solution.py:265
  306.0 4.1 all-to-all-start.6
  313.6 10.2 %all-to-all-done.6 = bf16[2,256,4,128]{3,1,0,2:T(8,128)(2,1)} async-done(((bf16[2,256,4,128]{3,1,0,2:T(8,128)(2,1)}), bf16[2,256,4,128]{3,1,0,2:T(8,128)(2,1)}, u32[]{:S(2)}, u32[]{:S(2)}) %all-to-all-start.6) | async-done | bytes 524320 | tf_op jit(solution)/shard_map/all_to_all | solution.py:288
  323.8 4.5 all-to-all-start.8
  333.4 27.0 %while.55 = (s32[]{:T(128)}, bf16[2,1024,2,64]{1,3,2,0:T(8,128)(2,1)}, bf16[2,1024,2,64]{1,3,2,0:T(8,128)(2,1)}, bf16[2,1024,2,64]{1,3,2,0:T(8,128)(2,1)}, bf16[...) while((s32[]{:T(128)}, ...), condition=%wide.region_25.26_spmd, body=%wide.region_23.25_spmd.sunk | while | flops 1377433600 | bytes 86582632 | solution.py:304
  335.4 3.0 multiply_reduce_fusion.14
  348.9 3.0 multiply_reduce_fusion.14
  363.2 5.0 copy.216
  368.2 5.1 all-to-all-start.7
  376.3 5.2 fusion.155
  381.5 3.5 fusion.150
  393.1 16.2 %all-to-all-done.7 = bf16[2,1024,3,1,128]{4,0,3,2,1:T(2,128)(2,1)} async-done(((bf16[2,1024,3,1,128]{4,0,3,2,1:T(2,128)(2,1)}), bf16[2,1024,3,1,128]{4,0,3,2,1:T(2,128)(2,1)}, u32[]{:S(2)}, u32[]{:S(2)}) %all-to-all-start.7) | async-done | bytes 1572896 | tf_op jit(solution)/shard_map/all_to_all | solution.py:310
  413.3 2.8 reshape.466
  419.6 40.1 %all-reduce = (f32[512]{0:T(512)}, f32[512]{0:T(512)}, f32[512]{0:T(512)}, f32[512]{0:T(512)}, f32[512]{0:T(512)}, /*index=5*/f32[512]{0:T(512)}) all-reduce(f32[512]{0:T(512)S(1)} %get-tuple-element.318, f32[512]{0:T(512)S(1)} %get-tuple-element.325, f32[512]{0:T(512)S(1)} %copy-done.71, ...), channel_id=1, replica_groups=mesh['dp'=8,'seq'=4] {'dp','seq'}, use_global_device_ids=true, to_apply=%region_34.35 | all-reduce | flops 3072 | bytes 24576 | tf_op jit(solution)/shard_map/psum | solution.py:317
  461.2 3.3 fusion.120
  464.5 3.8 convolution_add_fusion.3
  468.3 234.8 %all-reduce.4.cloned.1.call-done = (f32[512,1536]{0,1:T(8,128)}, f32[512,512]{1,0:T(8,128)}, f32[512,512]{1,0:T(8,128)}, f32[512,1024]{0,1:T(8,128)}, f32[512,51...) async-done(((f32[512,1536]{0,1:T(8,128)}, f32[512,512]{1,0:T(8,128)}, f32[512,512]{1,0:T(8,128)}, f32[512,1024]{0,1:T(8,128)}, f32[512,512]{1,0:T(8,128)}, ...) | async-done | bytes 16777232 | tf_op jit(solution)/shard_map/psum | solution.py:317
  703.1 3.7 copy.223
  (347 shorter events, 182.6 us)
Async XLA Ops:
  7.2 208.7 %copy-start = (bf16[512,2048]{1,0:T(8,128)(2,1)S(1)}, bf16[512,2048]{1,0:T(8,128)(2,1)}, u32[]{:S(2)}) copy-start(bf16[512,2048]{1,0:T(8,128)(2,1)} %param.36) | copy-start | bytes 6291460
  22.3 15.0 %collective-permute-start.2 = (bf16[2,256,3,1,128]{4,1,2,0,3:T(8,128)(2,1)}, bf16[2,256,3,1,128]{4,1,2,0,3:T(8,128)(2,1)S(1)}, u32[]{:S(2)}, u32[]{:S(2)}) collective-permute-start(bf16[2,256,3,1,128]{4,1,2,0,3:T(8,128)(2,1)} %bitcast.305), channel_id=1, source_target_pairs={{0,3},{1,0},{2,1},{3,2},{4,7},{5,4},{6,5},{7,6},{8,11},{9,8},{10,9... | collective-permute-start | bytes 1179656 | tf_op jit(solution)/shard_map/ppermute | solution.py:28
  28.2 33.0 %collective-permute-start.1 = (bf16[2,256,3,1,128]{4,1,2,0,3:T(8,128)(2,1)}, bf16[2,256,3,1,128]{4,1,2,0,3:T(8,128)(2,1)}, u32[]{:S(2)}, u32[]{:S(2)}) collective-permute-start(bf16[2,256,3,1,128]{4,1,2,0,3:T(8,128)(2,1)} %bitcast.306), channel_id=1, source_target_pairs={{0,2},{1,3},{2,0},{3,1},{4,6},{5,7},{6,4},{7,5},{8,10},{9,11},{10,... | collective-permute-start | bytes 1179656 | tf_op jit(solution)/shard_map/ppermute | solution.py:28
  29.0 32.2 %collective-permute-start = (bf16[2,256,3,1,128]{4,1,2,0,3:T(8,128)(2,1)}, bf16[2,256,3,1,128]{4,1,2,0,3:T(8,128)(2,1)}, u32[]{:S(2)}, u32[]{:S(2)}) collective-permute-start(bf16[2,256,3,1,128]{4,1,2,0,3:T(8,128)(2,1)} %bitcast.307), channel_id=1, source_target_pairs={{0,1},{1,2},{2,3},{3,0},{4,5},{5,6},{6,7},{7,4},{8,9},{9,10},{10,1... | collective-permute-start | bytes 1179656 | tf_op jit(solution)/shard_map/ppermute | solution.py:28
  70.7 7.2 copy-start.53
  96.3 13.8 %copy-start.56 = (f32[2,2,1024,1]{2,1,3,0:T(2,128)}, f32[2,2,1024,1]{2,1,3,0:T(2,128)S(1)}, u32[]{:S(2)}) copy-start(f32[2,2,1024,1]{2,1,3,0:T(2,128)S(1)} %get-tuple-element.784) | copy-start | bytes 49156
  98.3 20.4 %all-to-all-start = ((bf16[2,1024,1,128]{3,0,2,1:T(2,128)(2,1)}), bf16[2,1024,1,128]{3,0,2,1:T(2,128)(2,1)}, u32[]{:S(2)}, u32[]{:S(2)}) async-start(bf16[2,1024,1,128]{3,0,2,1:T(2,128)(2,1)} %copy.199), calls=%async_computation | async-start | bytes 1048576 | tf_op jit(solution)/shard_map/all_to_all | solution.py:175
  110.1 17.2 %copy-start.67 = (f32[512]{0:T(512)S(1)}, f32[512]{0:T(512)}, u32[]{:S(2)}) copy-start(f32[512]{0:T(512)} %param.38) | copy-start | bytes 6148
  110.1 17.2 %copy-start.73 = (f32[512]{0:T(512)S(1)}, f32[512]{0:T(512)}, u32[]{:S(2)}) copy-start(f32[512]{0:T(512)} %param.39) | copy-start | bytes 6148
  118.7 30.1 %all-to-all-start.1 = ((bf16[2,256,2,4,128]{4,2,1,0,3:T(2,128)(2,1)}), bf16[2,256,2,4,128]{4,2,1,0,3:T(2,128)(2,1)}, u32[]{:S(2)}, u32[]{:S(2)}) async-start(bf16[2,256,2,4,128]{4,2,1,0,3:T(2,128)(2,1)} %copy.202), calls=%async_computation.1 | async-start | bytes 2097152 | tf_op jit(solution)/shard_map/all_to_all | solution.py:159
  148.8 18.2 %all-to-all-start.2 = ((bf16[2,256,1,4,128]{4,1,0,2,3:T(8,128)(2,1)}), bf16[2,256,1,4,128]{4,1,0,2,3:T(8,128)(2,1)}, u32[]{:S(2)}, u32[]{:S(2)}) async-start(bf16[2,256,1,4,128]{4,1,0,2,3:T(8,128)(2,1)} %copy.204), calls=%async_computation.2 | async-start | bytes 1048576 | tf_op jit(solution)/shard_map/all_to_all | solution.py:193
  152.9 19.2 %copy-start.55 = (s32[2,1024]{1,0:T(2,128)S(1)}, s32[2,1024]{1,0:T(2,128)}, u32[]{:S(2)}) copy-start(s32[2,1024]{1,0:T(2,128)} %param.29) | copy-start | bytes 24580
  172.2 25.3 %copy-start.66 = (f32[512]{0:T(512)S(1)}, f32[512]{0:T(512)}, u32[]{:S(2)}) copy-start(f32[512]{0:T(512)} %param.42) | copy-start | bytes 6148
  192.7 23.1 %copy-start.62 = (f32[512]{0:T(512)S(1)}, f32[512]{0:T(512)}, u32[]{:S(2)}) copy-start(f32[512]{0:T(512)} %param.40) | copy-start | bytes 6148
  192.7 23.2 %copy-start.64 = (f32[512]{0:T(512)S(1)}, f32[512]{0:T(512)}, u32[]{:S(2)}) copy-start(f32[512]{0:T(512)} %param.41) | copy-start | bytes 6148
  192.7 18.8 %all-to-all-start.3 = ((bf16[2,1024,1,128]{3,0,2,1:T(2,128)(2,1)}), bf16[2,1024,1,128]{3,0,2,1:T(2,128)(2,1)}, u32[]{:S(2)}, u32[]{:S(2)}) async-start(bf16[2,1024,1,128]{3,0,2,1:T(2,128)(2,1)} %copy.206), calls=%async_computation.3 | async-start | bytes 1048576 | tf_op jit(solution)/shard_map/all_to_all | solution.py:206
  215.5 10.1 %copy-start.2 = (f32[512,512]{1,0:T(8,128)}, f32[512,512]{1,0:T(8,128)S(1)}, u32[]{:S(2)}) copy-start(f32[512,512]{1,0:T(8,128)S(1)} %get-tuple-element.439) | copy-start | bytes 3145732
  215.6 10.1 %copy-start.58 = (f32[512]{0:T(512)}, f32[512]{0:T(512)S(1)}, u32[]{:S(2)}) copy-start(f32[512]{0:T(512)S(1)} %broadcast_multiply_fusion.6) | copy-start | bytes 6148
  215.9 9.8 %copy-start.60 = (f32[512]{0:T(512)}, f32[512]{0:T(512)S(1)}, u32[]{:S(2)}) copy-start(f32[512]{0:T(512)S(1)} %add_rsqrt_fusion.1) | copy-start | bytes 6148
  226.1 29.7 %copy-start.8 = (f32[512,512]{1,0:T(8,128)}, f32[512,512]{1,0:T(8,128)S(1)}, u32[]{:S(2)}) copy-start(f32[512,512]{1,0:T(8,128)S(1)} %subtract_multiply_fusion.1) | copy-start | bytes 3145732
  226.1 30.6 %copy-start.4 = (bf16[2,1024,2,64]{1,3,2,0:T(8,128)(2,1)S(1)}, bf16[2,1024,2,64]{1,3,2,0:T(8,128)(2,1)}, u32[]{:S(2)}) copy-start(bf16[2,1024,2,64]{1,3,2,0:T(8,128)(2,1)} %get-tuple-element.842) | copy-start | bytes 1572868
  226.1 30.6 %copy-start.7 = (bf16[2,1024,2,64]{1,3,2,0:T(8,128)(2,1)S(1)}, bf16[2,1024,2,64]{1,3,2,0:T(8,128)(2,1)}, u32[]{:S(2)}) copy-start(bf16[2,1024,2,64]{1,3,2,0:T(8,128)(2,1)} %get-tuple-element.845) | copy-start | bytes 1572868
  231.3 18.4 %all-to-all-start.4 = ((bf16[2,256,4,128]{3,1,0,2:T(8,128)(2,1)}), bf16[2,256,4,128]{3,1,0,2:T(8,128)(2,1)}, u32[]{:S(2)}, u32[]{:S(2)}) async-start(bf16[2,256,4,128]{3,1,0,2:T(8,128)(2,1)} %copy.209), calls=%async_computation.4 | async-start | bytes 1048576 | tf_op jit(solution)/shard_map/all_to_all | solution.py:241
  265.3 4.1 copy-start.31
  283.8 18.3 %copy-start.9 = (f32[512,512]{1,0:T(8,128)S(1)}, f32[512,512]{1,0:T(8,128)}, u32[]{:S(2)}) copy-start(f32[512,512]{1,0:T(8,128)} %copy-done.8) | copy-start | bytes 3145732
  304.5 5.7 copy-start.11
  306.0 17.8 %all-to-all-start.6 = ((bf16[2,256,4,128]{3,1,0,2:T(8,128)(2,1)}), bf16[2,256,4,128]{3,1,0,2:T(8,128)(2,1)}, u32[]{:S(2)}, u32[]{:S(2)}) async-start(bf16[2,256,4,128]{3,1,0,2:T(8,128)(2,1)} %copy.214), calls=%async_computation.6 | async-start | bytes 1048576 | tf_op jit(solution)/shard_map/all_to_all | solution.py:288
  311.5 21.9 %copy-start.5 = (bf16[2,1024,2,64]{1,3,2,0:T(8,128)(2,1)S(1)}, bf16[2,1024,2,64]{1,3,2,0:T(8,128)(2,1)}, u32[]{:S(2)}) copy-start(bf16[2,1024,2,64]{1,3,2,0:T(8,128)(2,1)} %get-tuple-element.843) | copy-start | bytes 1572868
  311.5 21.9 %copy-start.6 = (bf16[2,1024,2,64]{1,3,2,0:T(8,128)(2,1)S(1)}, bf16[2,1024,2,64]{1,3,2,0:T(8,128)(2,1)}, u32[]{:S(2)}) copy-start(bf16[2,1024,2,64]{1,3,2,0:T(8,128)(2,1)} %get-tuple-element.844) | copy-start | bytes 1572868
  311.5 21.9 %copy-start.57 = (f32[2,2,1024,1]{2,1,3,0:T(2,128)S(1)}, f32[2,2,1024,1]{2,1,3,0:T(2,128)}, u32[]{:S(2)}) copy-start(f32[2,2,1024,1]{2,1,3,0:T(2,128)} %copy-done.56) | copy-start | bytes 49156
  323.8 44.4 %all-to-all-start.8 = ((bf16[2,1024,2,1,128]{4,0,3,2,1:T(2,128)(2,1)}), bf16[2,1024,2,1,128]{4,0,3,2,1:T(2,128)(2,1)}, u32[]{:S(2)}, u32[]{:S(2)}) async-start(bf16[2,1024,2,1,128]{4,0,3,2,1:T(2,128)(2,1)} %copy.219), calls=%async_computation.8 | async-start | bytes 2097152 | tf_op jit(solution)/shard_map/all_to_all | solution.py:272
  360.4 13.3 %copy-start.10 = (f32[512,512]{1,0:T(8,128)S(1)}, f32[512,512]{1,0:T(8,128)}, u32[]{:S(2)}) copy-start(f32[512,512]{1,0:T(8,128)} %copy-done.8) | copy-start | bytes 3145732
  363.2 13.0 %copy-start.3 = (f32[512,512]{1,0:T(8,128)S(1)}, f32[512,512]{1,0:T(8,128)}, u32[]{:S(2)}) copy-start(f32[512,512]{1,0:T(8,128)} %copy-done.2) | copy-start | bytes 3145732
  363.2 13.0 %copy-start.59 = (f32[512]{0:T(512)S(1)}, f32[512]{0:T(512)}, u32[]{:S(2)}) copy-start(f32[512]{0:T(512)} %copy-done.58) | copy-start | bytes 6148
  363.2 13.0 %copy-start.61 = (f32[512]{0:T(512)S(1)}, f32[512]{0:T(512)}, u32[]{:S(2)}) copy-start(f32[512]{0:T(512)} %copy-done.60) | copy-start | bytes 6148
  363.2 13.0 %copy-start.63 = (f32[512]{0:T(512)S(1)}, f32[512]{0:T(512)}, u32[]{:S(2)}) copy-start(f32[512]{0:T(512)} %param.40) | copy-start | bytes 6148
  363.2 13.0 %copy-start.65 = (f32[512]{0:T(512)S(1)}, f32[512]{0:T(512)}, u32[]{:S(2)}) copy-start(f32[512]{0:T(512)} %param.41) | copy-start | bytes 6148
  368.2 41.1 %all-to-all-start.7 = ((bf16[2,1024,3,1,128]{4,0,3,2,1:T(2,128)(2,1)}), bf16[2,1024,3,1,128]{4,0,3,2,1:T(2,128)(2,1)}, u32[]{:S(2)}, u32[]{:S(2)}) async-start(bf16[2,1024,3,1,128]{4,0,3,2,1:T(2,128)(2,1)} %copy.216), calls=%async_computation.7 | async-start | bytes 3145728 | tf_op jit(solution)/shard_map/all_to_all | solution.py:310
  373.3 329.8 %all-reduce.4.cloned.1.call-start = ((), (), s32[]{:S(2)}) async-start(), calls=%async_computation.9 | async-start | bytes 33554432 | tf_op jit(solution)/shard_map/psum | solution.py:317
  376.2 5.2 copy-start.24
  376.2 5.2 copy-start.51
  381.4 4.9 copy-start.28
  381.4 4.9 copy-start.74
  386.4 4.6 copy-start.54
  393.1 23.1 %copy-start.49 = (bf16[2,256,512]{2,1,0:T(8,128)(2,1)S(1)}, bf16[2,256,512]{2,1,0:T(8,128)(2,1)}, u32[]{:S(2)}) copy-start(bf16[2,256,512]{2,1,0:T(8,128)(2,1)} %param.26) | copy-start | bytes 1572868
  706.8 6.5 copy-start.52
  708.6 5.7 copy-start.26
  714.2 5.7 copy-start.1
  (62 other events, 127.0 us)
Sparse Core Ops, SparseCore 0:
  419.0 284.0 all-reduce.3
